TPU v7x, 32 devices: a whole 2x2x4 slice. The times are simulated.
32 devices in a mesh: groups: 2 (over y), seq: 4 (over z), res: 4 (over x, core).
Axes of the slice: x: 2, y: 2, z: 4, core: 2. Of those that a mesh axis runs over, the one named last changes fastest.
Arguments:
- alignment: float32 [256, 64, 64], P(('groups', 'seq'), 'res'), parts along dimension 0, may hold values from -100 to 100
- seq_mask: int32 [256, 64], P(('groups', 'seq'), 'res'), parts along dimension 0, may hold values from 0 to 1, as said below
- pair_rep: float32 [128, 64, 128], P(('groups', 'res'), 'seq'), parts along dimension 0, may hold values from -6 to 6
- chain_index: int32 [128], P('groups'), parts along dimension 0, may hold values from 0 to 3, never falling along the last dimension, each value on 1 to 32 neighbouring positions
- rel_table: float32 [66, 128], replicated, may hold values from -3 to 3
- w_factors: bfloat16 [64, 64], replicated, may hold values from -0.75 to 0.75
- w_outer: float32 [1024, 128], replicated, may hold values from -0.1875 to 0.1875
- w_bias: float32 [128, 8], replicated, may hold values from -1.5 to 1.5
- w_attention: bfloat16 [64, 256], replicated, may hold values from -30 to 30
- w_output: bfloat16 [64, 64], replicated, may hold values from -0.75 to 0.75
Outputs:
- pair_next: float32 [128, 64, 128], P(('groups', 'res'), 'seq'), parts along dimension 0
- alignment_next: float32 [256, 64, 64], P(('groups', 'seq'), 'res'), parts along dimension 0
There are 2 independent parts, one for each index of `groups`. A program takes and returns all parts, laid end to end along the dimension named above; an argument that names none is the same for every part. Nothing has to cross between parts.
Inputs may be any that keep to these rules, and one draw needn't show every extreme that they name: `seq_mask`: some residues at the end, at least the last one, are padding: 0 in every sequence. `chain_index`: chain index of a residue, never falling along the residues.
All inputs are finite; a program needn't handle non-finite values.
Results may differ from a plain program's by a relative error of at most 0.0015.
Values may be sent and summed in bfloat16 or wider, within the bound.
A program may use at most 64 MiB of HBM per device.

v0:
```python
import math

import jax
import jax.numpy as jnp
from jax import lax
from jax.sharding import PartitionSpec as P

EPSILON = 1e-05
PRECISE = lax.Precision.HIGHEST


def layer_norm(values):
    average = jnp.mean(values, -1, keepdims=True)
    centred = values - average
    variance = jnp.mean(centred * centred, -1, keepdims=True)
    return centred * lax.rsqrt(variance + EPSILON)


def block_size(total, limit):
    size = max(1, min(total, limit))
    while total % size:
        size -= 1
    return size


def body(
    alignment,
    seq_mask,
    pair_rep,
    chain_index,
    rel_table,
    w_factors,
    w_outer,
    w_bias,
    w_attention,
    w_output,
):
    seq_dev, res_dev, channels = alignment.shape
    col_block = pair_rep.shape[1]
    pair_width = pair_rep.shape[2]
    head_count = w_bias.shape[1]
    inner_width = w_attention.shape[1] // 4
    head_dim = inner_width // head_count
    factor_width = w_factors.shape[1] // 2
    row_start = lax.axis_index("res") * res_dev
    col_start = lax.axis_index("seq") * col_block
    mask_float = seq_mask.astype(jnp.float32)
    mask_half = seq_mask.astype(jnp.bfloat16)
    normed = layer_norm(alignment).astype(jnp.bfloat16)
    flattened = normed.reshape(seq_dev * res_dev, channels)
    projected = jnp.dot(flattened, w_factors, preferred_element_type=jnp.float32).reshape(
        seq_dev, res_dev, 2 * factor_width
    )
    left_factor = (projected[..., :factor_width] * mask_float[..., None]).astype(jnp.bfloat16)
    right_factor = (projected[..., factor_width:] * mask_float[..., None]).astype(jnp.bfloat16)
    features = jnp.dot(flattened, w_attention, preferred_element_type=jnp.float32).reshape(
        seq_dev, res_dev, 4 * inner_width
    )
    queries = features[..., :inner_width].astype(jnp.bfloat16)
    keys_local = features[..., inner_width : 2 * inner_width].astype(jnp.bfloat16)
    values_local = features[..., 2 * inner_width : 3 * inner_width].astype(jnp.bfloat16)
    gate_logits = features[..., 3 * inner_width :]
    right_all, keys_all, values_all, mask_all = (
        lax.all_gather(right_factor, "res", axis=1, tiled=True),
        lax.all_gather(keys_local, "res", axis=1, tiled=True),
        lax.all_gather(values_local, "res", axis=1, tiled=True),
        lax.all_gather(mask_half, "res", axis=1, tiled=True),
    )
    size = block_size(lax.axis_size("seq") * col_block, 48)
    grouped = right_all.reshape(
        seq_dev, lax.axis_size("seq") * col_block // size, size, factor_width
    ).transpose(1, 0, 2, 3)

    def one_block(right_block):
        outer_sum = jnp.einsum(
            "sic,sje->jice", left_factor, right_block, preferred_element_type=jnp.float32
        )
        flat_outer = outer_sum.reshape(size * res_dev, factor_width * factor_width)
        return jnp.dot(
            flat_outer, w_outer, precision=PRECISE, preferred_element_type=jnp.float32
        ).reshape(size, res_dev, pair_width)

    summed = lax.psum_scatter(
        lax.map(one_block, grouped).reshape(lax.axis_size("seq") * col_block, res_dev, pair_width),
        "seq",
        scatter_dimension=0,
        tiled=True,
    )
    count_terms = jnp.einsum("sj,si->ji", mask_all, mask_half, preferred_element_type=jnp.float32)
    counted = lax.psum_scatter(count_terms, "seq", scatter_dimension=0, tiled=True)
    update = jnp.transpose(summed, (1, 0, 2)) / jnp.maximum(counted.T, 1.0)[..., None]
    bin_count = rel_table.shape[0]
    reach = (bin_count - 2) // 2
    row_positions = row_start + jnp.arange(res_dev, dtype=jnp.int32)
    col_positions = col_start + jnp.arange(col_block, dtype=jnp.int32)
    row_chain = lax.dynamic_slice_in_dim(chain_index, row_start, res_dev)
    col_chain = lax.dynamic_slice_in_dim(chain_index, col_start, col_block)
    rel_bins = jnp.where(
        row_chain[:, None] == col_chain[None, :],
        jnp.clip(row_positions[:, None] - col_positions[None, :] + reach, 0, 2 * reach),
        2 * reach + 1,
    )
    one_hot = (rel_bins[..., None] == jnp.arange(bin_count, dtype=jnp.int32)).astype(jnp.float32)
    relative = jnp.dot(
        one_hot.reshape(res_dev * col_block, bin_count),
        rel_table,
        precision=PRECISE,
        preferred_element_type=jnp.float32,
    )
    pair_next = pair_rep + relative.reshape(res_dev, col_block, pair_width) + update
    pair_block = lax.all_gather(pair_next, "seq", axis=1, tiled=True)
    normed_pair = layer_norm(pair_block)
    head_values = jnp.dot(
        normed_pair.reshape(-1, pair_width),
        w_bias,
        precision=PRECISE,
        preferred_element_type=jnp.float32,
    )
    head_bias = head_values.reshape(res_dev, pair_block.shape[1], head_count).transpose(2, 0, 1)
    residues = keys_all.shape[1]
    group = block_size(seq_dev, max(1, 512 // res_dev))
    score_scale = 1.0 / math.sqrt(head_dim)

    def split_rows(tensor):
        return tensor.reshape((seq_dev // group, group) + tensor.shape[1:])

    def attend(block):
        query_block, key_block, value_block, gate_block, key_mask = block
        query_heads = query_block.reshape(group, res_dev, head_count, head_dim)
        key_heads = key_block.reshape(group, residues, head_count, head_dim)
        value_heads = value_block.reshape(group, residues, head_count, head_dim)
        scores = (
            jnp.einsum(
                "bihd,bjhd->bhij", query_heads, key_heads, preferred_element_type=jnp.float32
            )
            * score_scale
        )
        scores = (
            scores
            + head_bias[None]
            + 1000000000.0 * (key_mask.astype(jnp.float32)[:, None, None, :] - 1.0)
        )
        row_max = jnp.max(scores, -1, keepdims=True)
        weights = jnp.exp(scores - row_max)
        weights = (weights / jnp.sum(weights, -1, keepdims=True)).astype(jnp.bfloat16)
        attended = jnp.einsum(
            "bhij,bjhd->bihd", weights, value_heads, preferred_element_type=jnp.float32
        )
        attended = attended.reshape(group, res_dev, inner_width)
        return (jax.nn.sigmoid(gate_block) * attended).astype(jnp.bfloat16)

    gated = lax.map(
        attend,
        (
            split_rows(queries),
            split_rows(keys_all),
            split_rows(values_all),
            split_rows(gate_logits),
            split_rows(mask_all),
        ),
    )
    gated = gated.reshape(seq_dev * res_dev, inner_width)
    alignment_next = alignment + jnp.dot(
        gated, w_output, preferred_element_type=jnp.float32
    ).reshape(seq_dev, res_dev, channels)
    return (pair_next, alignment_next)


def solution(mesh):
    in_specs = (
        P(("groups", "seq"), "res", None),
        P(("groups", "seq"), "res"),
        P(("groups", "res"), "seq", None),
        P("groups"),
        P(),
        P(),
        P(),
        P(),
        P(),
        P(),
    )
    out_specs = (P(("groups", "res"), "seq", None), P(("groups", "seq"), "res", None))
    return jax.shard_map(body, mesh=mesh, in_specs=in_specs, out_specs=out_specs, check_vma=False)
```

profile of v0, /device:TPU:0, one launch (start us, length us, event | category | flops | bytes accessed | tf_op | source)
XLA Modules:
  0.0 129.0 jit_solution(1057264356791209544)
XLA Ops:
  7.2 0.0 copy-start
  7.2 0.0 reduce-scatter.5.cloned.1.call-start
  7.2 0.8 fusion.50
  8.0 6.2 %all_gather.16 = bf16[32,64]{0,1:T(8,128)(2,1)S(1)} all-gather(bf16[32,16]{0,1:T(8,128)(2,1)S(1)} %get-tuple-element.79), channel_id=1, replica_groups=mesh['groups'=2,'seq'=4,'res'=4] {'res'}, dimensions={1}, use_global_device_ids=true | all-gather | bytes 5120 | tf_op jit(solution)/shard_map/all_gather | solution.py:67
  14.2 0.7 fusion.58
  14.9 0.0 reduce-scatter.5.cloned.1.call-update
  14.9 0.0 reduce-scatter.3.cloned.1.call-start
  15.0 1.1 reduce_sum.46
  16.1 1.2 multiply_reduce_fusion.1
  17.3 1.1 multiply_convert_fusion
  18.5 0.9 fusion.27
  19.4 0.2 fusion.21
  19.6 7.6 %all_gather.15 = bf16[32,64,32]{2,0,1:T(8,128)(2,1)S(1)} all-gather(bf16[32,16,32]{2,0,1:T(8,128)(2,1)S(1)} %get-tuple-element.75), channel_id=1, replica_groups=mesh['groups'=2,'seq'=4,'res'=4] {'res'}, dimensions={1}, use_global_device_ids=true | all-gather | bytes 163840 | tf_op jit(solution)/shard_map/all_gather | solution.py:64
  27.2 0.3 copy.75
  27.5 0.0 copy-start.6
  27.5 45.5 %while.2 = (s32[]{:T(128)}, f32[2,32,16,128]{3,1,0,2:T(8,128)}, bf16[2,32,32,32]{1,3,2,0:T(8,128)(2,1)S(1)}, bf16[32,16,32]{2,0,1:T(8,128)(2,1)S(1)}, f32[1024,128]{1,0:T(8,128)S(1)}, /*index=5*/s32[]{:T(128)}) while((s32[]{:T(128)}, f32[2,32,16,128]{3,1,0,2:T(8,128)}, bf16[2,32,32,32]{1,3,2,0:T(8,128)(2,1)S(1)}, ...), condition=%wide.region_3.4_spmd, body=%wide.region_2.3_spmd.sunk | while | flops 838860800 | bytes 18481292 | solution.py:84
  27.5 4.4 %convolution_bitcast_fusion.6 = f32[32,16,32,32]{2,3,1,0:T(8,128)} fusion(bf16[2,32,32,32]{1,3,2,0:T(8,128)(2,1)S(1)} %get-tuple-element.134, s32[]{:T(128)S(6)} %copy.113, bf16[32,16,32]{2,0,1:T(8,128)(2,1)S(1)} %get-tuple-element.135), kind=kOutput, calls=%fused_computation.clone.1 | convolution fusion | flops 33554432 | bytes 2490372 | tf_op jit(solution)/shard_map/while/body/eval_jaxpr/sic,sje->jice/dot_general | solution.py:75
  32.0 9.0 %copy.109 = f32[32,16,32,32]{3,2,1,0:T(8,128)} copy(f32[32,16,32,32]{2,3,1,0:T(8,128)} %convolution_bitcast_fusion.6) | data formatting | bytes 4194304 | tf_op jit(solution)/shard_map/while/body/eval_jaxpr/sic,sje->jice/transpose | solution.py:75
  40.9 6.6 %reshape.201 = f32[32,16,1024]{2,1,0:T(8,128)S(1)} reshape(f32[32,16,32,32]{3,2,1,0:T(8,128)} %copy.109) | data formatting | bytes 4194304 | tf_op jit(solution)/shard_map/reshape.89
  47.6 0.0 copy-start.3
  47.6 1.8 %convolution_bitcast_fusion.7 = f32[1,32,16,128]{3,2,1,0:T(8,128)S(1)} fusion(f32[32,16,1024]{2,1,0:T(8,128)S(1)} %reshape.201, f32[1024,128]{1,0:T(8,128)S(1)} %get-tuple-element.136), kind=kOutput, calls=%fused_computation.1.clone.1 | convolution fusion | flops 805306368 | bytes 2883584 | tf_op jit(solution)/shard_map/while/body/eval_jaxpr/dot_general | solution.py:79
  49.4 0.0 copy-done.3
  49.4 0.1 copy_dynamic-update-slice_fusion.2
  49.5 0.8 copy-done.4
  50.3 4.4 %convolution_bitcast_fusion.6 = f32[32,16,32,32]{2,3,1,0:T(8,128)} fusion(bf16[2,32,32,32]{1,3,2,0:T(8,128)(2,1)S(1)} %get-tuple-element.134, s32[]{:T(128)S(6)} %copy.113, bf16[32,16,32]{2,0,1:T(8,128)(2,1)S(1)} %get-tuple-element.135), kind=kOutput, calls=%fused_computation.clone.1 | convolution fusion | flops 33554432 | bytes 2490372 | tf_op jit(solution)/shard_map/while/body/eval_jaxpr/sic,sje->jice/dot_general | solution.py:75
  54.7 9.0 %copy.109 = f32[32,16,32,32]{3,2,1,0:T(8,128)} copy(f32[32,16,32,32]{2,3,1,0:T(8,128)} %convolution_bitcast_fusion.6) | data formatting | bytes 4194304 | tf_op jit(solution)/shard_map/while/body/eval_jaxpr/sic,sje->jice/transpose | solution.py:75
  63.7 6.6 %reshape.201 = f32[32,16,1024]{2,1,0:T(8,128)S(1)} reshape(f32[32,16,32,32]{3,2,1,0:T(8,128)} %copy.109) | data formatting | bytes 4194304 | tf_op jit(solution)/shard_map/reshape.89
  70.3 1.8 %convolution_bitcast_fusion.7 = f32[1,32,16,128]{3,2,1,0:T(8,128)S(1)} fusion(f32[32,16,1024]{2,1,0:T(8,128)S(1)} %reshape.201, f32[1024,128]{1,0:T(8,128)S(1)} %get-tuple-element.136), kind=kOutput, calls=%fused_computation.1.clone.1 | convolution fusion | flops 805306368 | bytes 2883584 | tf_op jit(solution)/shard_map/while/body/eval_jaxpr/dot_general | solution.py:79
  72.1 0.1 copy_dynamic-update-slice_fusion.2
  72.3 0.0 copy-start.4
  72.3 0.8 copy-done.4
  73.0 0.0 reduce-scatter.3.cloned.1.call-update
  73.1 0.1 copy.83
  73.2 0.0 copy-done.6
  73.2 0.2 fusion.52
  73.4 0.1 fusion.49
  73.5 0.0 copy-start.9
  73.5 0.0 copy-start.10
  73.5 7.4 %all_gather.18 = bf16[32,64,64]{2,1,0:T(8,128)(2,1)S(1)} all-gather(bf16[32,16,64]{2,1,0:T(8,128)(2,1)S(1)} %get-tuple-element.77), channel_id=1, replica_groups=mesh['groups'=2,'seq'=4,'res'=4] {'res'}, dimensions={1}, use_global_device_ids=true | all-gather | bytes 327680 | tf_op jit(solution)/shard_map/all_gather | solution.py:65
  80.9 0.3 copy.80
  81.2 0.3 copy.90
  81.5 0.0 copy-start.8
  81.5 7.3 %all_gather.17 = bf16[32,64,64]{2,1,0:T(8,128)(2,1)S(1)} all-gather(bf16[32,16,64]{2,1,0:T(8,128)(2,1)S(1)} %get-tuple-element.76), channel_id=1, replica_groups=mesh['groups'=2,'seq'=4,'res'=4] {'res'}, dimensions={1}, use_global_device_ids=true | all-gather | bytes 327680 | tf_op jit(solution)/shard_map/all_gather | solution.py:66
  88.8 0.3 copy.78
  89.1 0.1 fusion.51
  89.2 0.1 clamp_select_fusion
  89.3 0.0 reduce-scatter.5.cloned.1.call-done
  89.3 0.7 maximum_bitcast_fusion
  90.0 0.1 copy.77
  90.1 6.1 %reduce-scatter.3.cloned.1.call-done = f32[16,16,128]{2,0,1:T(8,128)} async-done(((f32[64,16,128]{2,0,1:T(8,128)}), f32[16,16,128]{2,0,1:T(8,128)}) %reduce-scatter.3.cloned.1.call-update) | async-done | bytes 131088 | tf_op jit(solution)/shard_map/reduce_scatter | solution.py:83
  96.2 1.2 fusion.7
  97.4 0.0 copy-start.5
  97.4 16.0 %all_gather.19 = f32[16,64,128]{2,1,0:T(8,128)S(1)} all-gather(f32[16,16,128]{2,1,0:T(8,128)S(1)} %fusion.7), channel_id=1, replica_groups=mesh['groups'=2,'seq'=4,'res'=4] {'seq'}, dimensions={1}, use_global_device_ids=true | all-gather | bytes 655360 | tf_op jit(solution)/shard_map/all_gather | solution.py:111
  113.4 0.2 reduce_sum.48
  113.6 0.4 multiply_reduce_fusion
  114.1 1.5 %convolution_bitcast_fusion.3 = f32[8,16,64]{2,0,1:T(8,128)S(1)} fusion(f32[16,64,128]{2,1,0:T(8,128)S(1)} %all_gather.19, f32[16,64]{1,0:T(8,128)S(1)} %add_rsqrt_fusion.1, f32[16,64]{1,0:T(8,128)S(1)} %broadcast_multiply_fusion.1, f32[128,8]{0,1:T(8,128)S(1)} %copy-done.8), kind=kOutput, calls=%fused_computation.17 | convolution fusion | flops 12845056 | bytes 569344 | tf_op jit(solution)/shard_map/dot_general | solution.py:113
  115.6 2.4 %fusion.53 = (f32[32,8,16]{2,1,0:T(8,128)S(1)}, f32[32,8,16,64]{3,2,1,0:T(8,128)}) fusion(f32[32,64]{1,0:T(8,128)S(1)} %add_multiply_fusion, f32[8,16,64]{2,1,0:T(8,128)S(1)} %copy.82, bf16[32,64,64]{1,2,0:T(8,128)(2,1)S(1)} %copy.80, bf16[32,16,64]{1,2,0:T(8,128)(2,1)S(1)} %copy.90), kind=kOutput, calls=%fused_computation.68 | convolution fusion | flops 5505087 | bytes 1433600 | tf_op jit(solution)/shard_map/while/body/eval_jaxpr/sub | solution.py:144
  117.9 2.2 %convolution_bitcast_fusion.2 = f32[32,16,64]{1,2,0:T(8,128)S(1)} fusion(f32[32,8,16,64]{3,2,1,0:T(8,128)} %get-tuple-element.86, f32[32,8,16]{2,1,0:T(8,128)S(1)} %get-tuple-element.85, bf16[32,64,64]{1,2,0:T(8,128)(2,1)S(1)} %copy.78), kind=kOutput, calls=%fused_computation.13 | convolution fusion | flops 4718592 | bytes 1458176 | tf_op jit(solution)/shard_map/while/body/eval_jaxpr/bhij,bjhd->bihd/dot_general | solution.py:146
  120.2 0.0 copy-start.2
  120.2 0.3 copy.85
  120.5 0.2 fusion.25
  120.7 0.4 copy-done.2
  121.1 0.2 convolution_add_fusion
  121.3 0.9 copy.88
  (20 shorter events, 0.1 us)
Async XLA Ops:
  7.2 89.0 %copy-start = (f32[66,128]{1,0:T(8,128)S(1)}, f32[66,128]{1,0:T(8,128)}, u32[]{:S(2)}) copy-start(f32[66,128]{1,0:T(8,128)} %param.16) | copy-start | bytes 101380
  7.2 20.3 %copy-start.1 = (f32[1024,128]{1,0:T(8,128)S(1)}, f32[1024,128]{1,0:T(8,128)}, u32[]{:S(2)}) copy-start(f32[1024,128]{1,0:T(8,128)} %param.18) | copy-start | bytes 1572868
  7.2 82.1 %reduce-scatter.5.cloned.1.call-start = ((), (), s32[]{:S(2)}) async-start(), calls=%async_computation.3 | async-start | bytes 40960 | tf_op jit(solution)/shard_map/reduce_scatter | solution.py:90
  14.9 81.3 %reduce-scatter.3.cloned.1.call-start = ((), (), s32[]{:S(2)}) async-start(), calls=%async_computation.2 | async-start | bytes 655360 | tf_op jit(solution)/shard_map/reduce_scatter | solution.py:83
  27.5 45.7 %copy-start.6 = (bf16[64,256]{1,0:T(8,128)(2,1)S(1)}, bf16[64,256]{1,0:T(8,128)(2,1)}, u32[]{:S(2)}) copy-start(bf16[64,256]{1,0:T(8,128)(2,1)} %param.20) | copy-start | bytes 98308
  47.6 1.8 %copy-start.3 = (f32[2,32,16,128]{3,1,0,2:T(8,128)S(1)}, f32[2,32,16,128]{3,1,0,2:T(8,128)}, u32[]{:S(2)}) copy-start(f32[2,32,16,128]{3,1,0,2:T(8,128)} %get-tuple-element.127) | copy-start | bytes 1572868 | tf_op jit(solution)/shard_map/while
  49.5 0.8 copy-start.4
  70.3 1.8 %copy-start.3 = (f32[2,32,16,128]{3,1,0,2:T(8,128)S(1)}, f32[2,32,16,128]{3,1,0,2:T(8,128)}, u32[]{:S(2)}) copy-start(f32[2,32,16,128]{3,1,0,2:T(8,128)} %get-tuple-element.127) | copy-start | bytes 1572868 | tf_op jit(solution)/shard_map/while
  72.3 0.8 copy-start.4
  73.5 15.6 %copy-start.9 = (s32[64]{0:T(128)S(1)}, s32[64]{0:T(128)}, u32[]{:S(2)}) copy-start(s32[64]{0:T(128)} %param.15) | copy-start | bytes 772
  73.5 22.7 %copy-start.10 = (f32[16,16,128]{2,1,0:T(8,128)S(1)}, f32[16,16,128]{2,1,0:T(8,128)}, u32[]{:S(2)}) copy-start(f32[16,16,128]{2,1,0:T(8,128)} %param.14) | copy-start | bytes 393220
  81.5 32.5 %copy-start.8 = (f32[128,8]{0,1:T(8,128)S(1)}, f32[128,8]{0,1:T(8,128)}, u32[]{:S(2)}) copy-start(f32[128,8]{0,1:T(8,128)} %param.19) | copy-start | bytes 12292
  97.4 20.6 %copy-start.5 = (f32[16,16,128]{2,1,0:T(8,128)}, f32[16,16,128]{2,1,0:T(8,128)S(1)}, u32[]{:S(2)}) copy-start(f32[16,16,128]{2,1,0:T(8,128)S(1)} %fusion.7) | copy-start | bytes 393220
  117.9 2.7 %copy-start.7 = (bf16[64,64]{1,0:T(8,128)(2,1)S(1)}, bf16[64,64]{1,0:T(8,128)(2,1)}, u32[]{:S(2)}) copy-start(bf16[64,64]{1,0:T(8,128)(2,1)} %param.21) | copy-start | bytes 24580
  120.2 1.0 copy-start.2
Sparse Core Ops, SparseCore 0:
  15.1 20.5 reduce-scatter.4
  73.2 22.9 reduce-scatter.2
where the time goes:
time: 130 us; the launch traced here: 129 us
  blocking collectives  44.5 us (34%)
  local copies, waits for them, and re-layouts  36.1 us (28%)
  matrix products  21.7 us (17%)
  between operations  14.3 us (11%)
  waiting for transfers between devices  6.16 us (5%)
  other arithmetic  5.99 us (5%)
    transpose x2, local copies, waits for them, and re-layouts, one_block(): jnp.einsum('sic,sje->jice', left_factor, right_block, preferred_element_t...  17.9 us
    all_gather x1, blocking collectives, body(): pair_block = lax.all_gather(pair_next, 'seq', axis=1, tiled=True)  16 us
    another operation x2, local copies, waits for them, and re-layouts  13.3 us
    dot_general x2, matrix products, one_block(): jnp.einsum('sic,sje->jice', left_factor, right_block, preferred_element_t...  8.88 us
    all_gather x1, blocking collectives, body(): lax.all_gather(right_factor, 'res', axis=1, tiled=True)  7.62 us
    all_gather x1, blocking collectives, body(): lax.all_gather(keys_local, 'res', axis=1, tiled=True)  7.43 us
    all_gather x1, blocking collectives, body(): lax.all_gather(values_local, 'res', axis=1, tiled=True)  7.29 us
    all_gather x1, blocking collectives, body(): lax.all_gather(mask_half, 'res', axis=1, tiled=True)  6.17 us
  transfers between devices with their start and end apart: 2, of which 1 were waited for; matrix products, arithmetic and copies ran while one was open for 39% of the time, Pallas kernels for 0%

commit v1 on v0

v1 whole, which is shorter than its diff:
```python
import functools
import math

import jax
import jax.numpy as jnp
from jax import lax
from jax.experimental import pallas as pl
from jax.experimental.pallas import tpu as pltpu
from jax.sharding import PartitionSpec as P

EPSILON = 1e-05
PRECISE = lax.Precision.HIGHEST
MESH = pl.DeviceIdType.MESH
F32 = jnp.float32
BF16 = jnp.bfloat16
LANES = 128


def iota(shape, dim):
    return lax.broadcasted_iota(jnp.int32, shape, dim)


def dot(a, b, dims=((1,), (0,)), precision=None):
    return lax.dot_general(
        a, b, (dims, ((), ())), precision=precision, preferred_element_type=F32
    )


def layer_norm(values):
    average = jnp.mean(values, -1, keepdims=True)
    centred = values - average
    variance = jnp.mean(centred * centred, -1, keepdims=True)
    return centred * lax.rsqrt(variance + EPSILON)


def split(values):
    high = values.astype(BF16)
    return high, (values - high.astype(F32)).astype(BF16)


def kernel(
    n_seq,
    n_res,
    sizes,
    align_ref,
    mask_ref,
    pair_ref,
    chain_ref,
    table_ref,
    wf_ref,
    wo_ref,
    wb_ref,
    wa_ref,
    wout_ref,
    pair_out,
    align_out,
    x_scr,
    left_buf,
    right_buf,
    right_own,
    x_buf,
    mask_buf,
    bias_buf,
    bias_own,
    bias_scr,
    base_scr,
    wsplit,
    wa_diag,
    qk_scr,
    vg_scr,
    q_scr,
    gate_scr,
    outer_scr,
    lhs_high,
    lhs_low,
    att_scr,
    score_scr,
    send_l,
    recv_l,
    send_r,
    recv_r,
    send_x,
    recv_x,
    send_m,
    recv_m,
    send_b,
    recv_b,
):
    sd, rd, ch, cb, cz, co, heads, hd, bins = sizes
    inner = heads * hd
    ratio = rd // cb
    rows = sd * rd
    pairs = rd * cb
    residues = n_res * rd
    fl = rd * co
    q = lax.axis_index("seq")
    r = lax.axis_index("res")
    owner = q // ratio
    diagonal = (owner == r).astype(jnp.int32)

    barrier = pltpu.get_barrier_semaphore()
    seq_peers = [lax.rem(q + d, n_seq) for d in range(n_seq)]
    res_peers = [lax.rem(r + d, n_res) for d in range(n_res)]
    for d in range(1, n_seq):
        pl.semaphore_signal(
            barrier, inc=1, device_id={"seq": seq_peers[d], "res": r}, device_id_type=MESH
        )
    for d in range(1, n_res):
        pl.semaphore_signal(
            barrier, inc=1, device_id={"seq": q, "res": res_peers[d]}, device_id_type=MESH
        )
    for d in range(n_seq):

        def greet(d=d):
            pl.semaphore_signal(
                barrier, inc=1, device_id={"seq": seq_peers[d], "res": owner}, device_id_type=MESH
            )

        if d == 0:
            pl.when(owner != r)(greet)
        else:
            greet()

    normed = layer_norm(align_ref[...])
    x_scr[...] = normed
    half = rows // 2
    x_buf[r] = jnp.concatenate([normed[:half], normed[half:]], axis=1).astype(BF16)
    mask = mask_ref[...].astype(F32)
    eye = (iota((rd, rd), 0) == iota((rd, rd), 1)).astype(BF16)
    mask_turned = dot(eye, mask.astype(BF16), ((1,), (1,)))
    mask_wide = jnp.concatenate([mask_turned, jnp.zeros((rd, LANES - sd), F32)], axis=1)
    mask_buf[r] = mask_wide
    wf = wf_ref[...]
    wf_wide = jnp.concatenate([wf, wf], axis=1)
    per = LANES // co
    lane_block = iota((sd, LANES), 1) // co
    for g in range(rd // per):
        left = jnp.zeros((sd, LANES), F32)
        right = jnp.zeros((sd, LANES), F32)
        for m in range(per):
            i = g * per + m
            factor = dot(x_scr[pl.ds(i, sd, stride=rd), :].astype(BF16), wf_wide)
            factor = factor * mask[:, i : i + 1]
            left_at = (co * m) % LANES
            right_at = (co * m - co) % LANES
            left = jnp.where(lane_block == m, pltpu.roll(factor, left_at, 1) if left_at else factor, left)
            right = jnp.where(
                lane_block == m, pltpu.roll(factor, right_at, 1) if right_at else factor, right
            )
        left_buf[q, :, g * LANES : (g + 1) * LANES] = left.astype(BF16)
        right_own[:, g * LANES : (g + 1) * LANES] = right.astype(BF16)
    mask_pad = jnp.concatenate([mask, jnp.zeros((sd, LANES - rd), F32)], axis=1).astype(BF16)
    left_buf[q, :, fl : fl + LANES] = mask_pad
    right_own[:, fl : fl + LANES] = mask_pad

    pl.semaphore_wait(barrier, (n_seq - 1) + (n_res - 1) + ratio * n_res - diagonal)

    def right_copy(t, d):
        return pltpu.make_async_remote_copy(
            src_ref=right_own,
            dst_ref=right_buf.at[q],
            send_sem=send_r.at[t * n_res + d],
            recv_sem=recv_r.at[q],
            device_id={"seq": r * ratio + t, "res": res_peers[d]},
            device_id_type=MESH,
        )

    def left_copy(d):
        return pltpu.make_async_remote_copy(
            src_ref=left_buf.at[q],
            dst_ref=left_buf.at[q],
            send_sem=send_l.at[d],
            recv_sem=recv_l.at[d],
            device_id={"seq": seq_peers[d], "res": r},
            device_id_type=MESH,
        )

    def x_copy(d):
        return pltpu.make_async_remote_copy(
            src_ref=x_buf.at[r],
            dst_ref=x_buf.at[r],
            send_sem=send_x.at[d],
            recv_sem=recv_x.at[d],
            device_id={"seq": q, "res": res_peers[d]},
            device_id_type=MESH,
        )

    def mask_copy(d):
        return pltpu.make_async_remote_copy(
            src_ref=mask_buf.at[r],
            dst_ref=mask_buf.at[r],
            send_sem=send_m.at[d],
            recv_sem=recv_m.at[d],
            device_id={"seq": q, "res": res_peers[d]},
            device_id_type=MESH,
        )

    def each_right(action):
        for t in range(ratio):
            for d in range(n_res):
                if d == 0:
                    pl.when(r * ratio + t != q)(functools.partial(action, t, d))
                else:
                    action(t, d)

    each_right(lambda t, d: right_copy(t, d).start())
    for d in range(1, n_seq):
        left_copy(d).start()
    for d in range(1, n_res):
        x_copy(d).start()
        mask_copy(d).start()

    @pl.when(owner == r)
    def _():
        right_buf[q] = right_own[...]

    wo_high, wo_low = split(wo_ref[...])
    wsplit[:, :cz] = wo_high
    wsplit[:, cz:] = wo_low
    wa_diag[...] = jnp.zeros_like(wa_diag)
    wa_diag[:ch, : 4 * inner] = wa_ref[...]
    wa_diag[ch:, 4 * inner :] = wa_ref[...]

    row = iota((rd, LANES), 0)
    lane = iota((rd, LANES), 1)
    reach = (bins - 2) // 2
    row_chain = jnp.zeros((rd, LANES), jnp.int32)
    for i in range(rd):
        row_chain = jnp.where(row == i, chain_ref[r * rd + i], row_chain)
    tab_high, tab_low = split(
        jnp.concatenate([table_ref[...], jnp.zeros((LANES - bins, cz), F32)], axis=0)
    )
    hot = []
    for j in range(cb):
        column = q * cb + j
        bin_ = jnp.where(
            row_chain == chain_ref[column],
            jnp.clip(row + r * rd - column + reach, 0, 2 * reach),
            2 * reach + 1,
        )
        hot.append(jnp.where(lane == bin_, 1.0, 0.0).astype(BF16))
    hot = jnp.concatenate(hot, axis=0)
    relative = dot(hot, tab_high) + dot(hot, tab_low)
    for j in range(cb):
        base_scr[j * rd : (j + 1) * rd] = (
            pair_ref[pl.ds(j, rd, stride=cb), :] + relative[j * rd : (j + 1) * rd]
        )

    spread = (iota((heads, LANES), 1) // rd == iota((heads, LANES), 0)).astype(F32)
    wb_high, wb_low = split(dot(wb_ref[...], spread, precision=PRECISE))
    wb_both = jnp.concatenate([wb_high, wb_low], axis=1)

    def project(block):
        features = dot(x_buf[block], wa_diag[...])
        for part in range(2):
            at = 4 * inner * part
            qk_scr[block, part * half : (part + 1) * half] = features[:, at : at + LANES].astype(BF16)
            vg_scr[block, part * half : (part + 1) * half] = features[
                :, at + LANES : at + 2 * LANES
            ].astype(BF16)
        return features

    own = project(r)
    for part in range(2):
        at = 4 * inner * part
        place = slice(part * half, (part + 1) * half)
        q_scr[place] = pltpu.roll(own[:, at : at + LANES], inner, 1).astype(BF16)
        gate_scr[place] = jax.nn.sigmoid(
            pltpu.roll(own[:, at + LANES : at + 2 * LANES], inner, 1)
        )

    for d in range(1, n_seq):
        left_copy(d).wait_recv()
    for source in range(n_seq):

        def arrive(source=source):
            pltpu.make_async_remote_copy(
                src_ref=right_own,
                dst_ref=right_buf.at[source],
                send_sem=send_r.at[0],
                recv_sem=recv_r.at[source],
                device_id={"seq": source, "res": owner},
                device_id_type=MESH,
            ).wait_recv()

        pl.when(jnp.logical_or(owner != r, q != source))(arrive)

    left_all = left_buf[:, :, :fl].reshape(n_seq * sd, fl)
    block = iota((rd, LANES), 1) // co
    block_tall = jnp.concatenate([block] * (co // per), axis=0)
    for g in range(cb // per):
        at = g * LANES
        if ratio > 1:
            at = pl.multiple_of(lax.rem(q, ratio) * (cb * co) + g * LANES, LANES)
        right_part = right_buf[:, :, pl.ds(at, LANES)].reshape(n_seq * sd, LANES)
        outer_scr[g] = dot(left_all, right_part, ((0,), (0,)))
        tall = [
            jnp.concatenate(
                [outer_scr[g, pl.ds(per * k + m, rd, stride=co), :] for k in range(co // per)], axis=0
            )
            for m in range(per)
        ]
        for jj in range(per):
            total = None
            for m in range(per):
                shift = (co * (m - jj)) % LANES
                moved = pltpu.roll(tall[m], shift, 1) if shift else tall[m]
                total = moved if total is None else jnp.where(block_tall == m, moved, total)
            high, low = split(total)
            place = slice((g * per + jj) * rd, (g * per + jj + 1) * rd)
            for k in range(co // per):
                lhs_high[place, k * LANES : (k + 1) * LANES] = high[k * rd : (k + 1) * rd]
                lhs_low[place, k * LANES : (k + 1) * LANES] = low[k * rd : (k + 1) * rd]
    both = dot(lhs_high[...], wsplit[...])
    update = both[:, :cz] + both[:, cz:] + dot(lhs_low[...], wsplit[:, :cz])
    counted = dot(
        left_buf[:, :, fl : fl + LANES].reshape(n_seq * sd, LANES),
        right_buf[:, :, fl : fl + LANES].reshape(n_seq * sd, LANES),
        ((0,), (0,)),
    )[:rd]
    if ratio > 1:
        counted = pltpu.roll(counted, LANES - lax.rem(q, ratio) * cb, 1)
    scale = 1.0 / jnp.maximum(counted, 1.0)
    scale = jnp.concatenate(
        [jnp.broadcast_to(scale[:, j : j + 1], (rd, LANES)) for j in range(cb)], axis=0
    )
    pair_next = base_scr[...] + update * scale
    for j in range(cb):
        pair_out[pl.ds(j, rd, stride=cb), :] = pair_next[j * rd : (j + 1) * rd]
    n_high, n_low = split(layer_norm(pair_next))
    both = dot(n_high, wb_both)
    head = both[:, :LANES] + both[:, LANES:] + dot(n_low, wb_high)
    keep = iota((pairs, LANES), 0) % rd == iota((pairs, LANES), 1) % rd
    head = jnp.where(keep, head, 0.0).reshape(cb, rd, LANES)
    bias_own[:cb] = jnp.sum(head, axis=1)

    def bias_copy(d):
        return pltpu.make_async_remote_copy(
            src_ref=bias_own,
            dst_ref=bias_buf.at[q],
            send_sem=send_b.at[d],
            recv_sem=recv_b.at[d],
            device_id={"seq": seq_peers[d], "res": r},
            device_id_type=MESH,
        )

    for d in range(1, n_seq):
        bias_copy(d).start()
    bias_buf[q] = bias_own[...]

    for d in range(1, n_res):
        x_copy(d).wait_recv()
        mask_copy(d).wait_recv()
    for d in range(1, n_res):
        project(lax.rem(r + n_res - d, n_res))
    wide = heads * rd
    wide_row = iota((wide, LANES), 0) // rd
    wide_lane = iota((wide, LANES), 1)
    query_mask = jnp.where((wide_lane - inner) // hd == wide_row, 1.0, 0.0)
    query_mask = jnp.where(wide_lane >= inner, query_mask, 0.0).astype(BF16)
    out_mask = wide_lane // hd == wide_row
    score_scale = 1.0 / math.sqrt(hd)
    for s in range(sd):
        at = slice(s * rd, (s + 1) * rd)
        keys = qk_scr[:, at].reshape(residues, LANES)
        queries = jnp.concatenate([q_scr[at]] * heads, axis=0) * query_mask
        score_scr[s] = dot(keys, queries, ((1,), (1,))) * score_scale
    mask_bias = 1000000000.0 * (mask_buf[...].reshape(residues, LANES) - 1.0)

    for d in range(1, n_seq):
        bias_copy(d).wait_recv()
    for j in range(n_seq):
        bias_scr[j * cb : (j + 1) * cb] = bias_buf[j, :cb]
    bias = bias_scr[...]
    for s in range(sd):
        at = slice(s * rd, (s + 1) * rd)
        scores = score_scr[s] + bias + mask_bias[:, s : s + 1]
        weights = jnp.exp(scores - jnp.max(scores, 0, keepdims=True))
        weights = (weights * (1.0 / jnp.sum(weights, 0, keepdims=True))).astype(BF16)
        values = vg_scr[:, at].reshape(residues, LANES)
        mixed = jnp.where(out_mask, dot(weights, values, ((0,), (0,))), 0.0)
        att_scr[at] = jnp.sum(mixed.reshape(heads, rd, LANES), axis=0)
    gated = (gate_scr[...] * att_scr[...]).astype(BF16)[:, :inner]
    align_out[...] = align_ref[...] + dot(gated, wout_ref[...])

    each_right(lambda t, d: right_copy(t, d).wait_send())
    for d in range(1, n_seq):
        left_copy(d).wait_send()
        bias_copy(d).wait_send()
    for d in range(1, n_res):
        x_copy(d).wait_send()
        mask_copy(d).wait_send()


def solution(mesh):
    n_seq, n_res = mesh.shape["seq"], mesh.shape["res"]

    def body(align, mask, pair, chain, table, w_factors, w_outer, w_bias, w_attention, w_output):
        sd, rd, ch = align.shape
        cb, cz = pair.shape[1:]
        co = w_factors.shape[1] // 2
        heads = w_bias.shape[1]
        inner = w_attention.shape[1] // 4
        bins = table.shape[0]
        rows, pairs, residues = sd * rd, rd * cb, n_res * rd
        fl = rd * co
        per = LANES // co
        slot = max(cb, 8)
        sizes = (sd, rd, ch, cb, cz, co, heads, inner // heads, bins)
        vmem = pl.BlockSpec(memory_space=pltpu.VMEM)
        smem = pl.BlockSpec(memory_space=pltpu.SMEM)
        dma = pltpu.SemaphoreType.DMA
        pair_next, align_next = pl.pallas_call(
            functools.partial(kernel, n_seq, n_res, sizes),
            out_shape=(
                jax.ShapeDtypeStruct((pairs, cz), F32),
                jax.ShapeDtypeStruct((rows, ch), F32),
            ),
            in_specs=[vmem, vmem, vmem, smem] + [vmem] * 6,
            out_specs=(vmem, vmem),
            scratch_shapes=[
                pltpu.VMEM((rows, ch), F32),
                pltpu.VMEM((n_seq, sd, fl + LANES), BF16),
                pltpu.VMEM((n_seq, sd, fl + LANES), BF16),
                pltpu.VMEM((sd, fl + LANES), BF16),
                pltpu.VMEM((n_res, rows // 2, 2 * ch), BF16),
                pltpu.VMEM((n_res, rd, LANES), F32),
                pltpu.VMEM((n_seq, slot, LANES), F32),
                pltpu.VMEM((slot, LANES), F32),
                pltpu.VMEM((residues, LANES), F32),
                pltpu.VMEM((pairs, cz), F32),
                pltpu.VMEM((co * co, 2 * cz), BF16),
                pltpu.VMEM((2 * ch, 8 * inner), BF16),
                pltpu.VMEM((n_res, rows, LANES), BF16),
                pltpu.VMEM((n_res, rows, LANES), BF16),
                pltpu.VMEM((rows, LANES), BF16),
                pltpu.VMEM((rows, LANES), F32),
                pltpu.VMEM((cb // per, fl, LANES), F32),
                pltpu.VMEM((pairs, co * co), BF16),
                pltpu.VMEM((pairs, co * co), BF16),
                pltpu.VMEM((rows, LANES), F32),
                pltpu.VMEM((sd, residues, LANES), F32),
                dma((n_seq,)),
                dma((n_seq,)),
                dma((rd // cb * n_res,)),
                dma((n_seq,)),
                dma((n_res,)),
                dma((n_res,)),
                dma((n_res,)),
                dma((n_res,)),
                dma((n_seq,)),
                dma((n_seq,)),
            ],
            compiler_params=pltpu.CompilerParams(
                collective_id=0, has_side_effects=True, vmem_limit_bytes=48 * 1024 * 1024
            ),
        )(
            align.reshape(rows, ch),
            mask,
            pair.reshape(pairs, cz),
            chain,
            table,
            w_factors,
            w_outer,
            w_bias,
            w_attention,
            w_output,
        )
        return pair_next.reshape(rd, cb, cz), align_next.reshape(sd, rd, ch)

    in_specs = (
        P(("groups", "seq"), "res", None),
        P(("groups", "seq"), "res"),
        P(("groups", "res"), "seq", None),
        P("groups"),
        P(),
        P(),
        P(),
        P(),
        P(),
        P(),
    )
    out_specs = (P(("groups", "res"), "seq", None), P(("groups", "seq"), "res", None))
    return jax.shard_map(body, mesh=mesh, in_specs=in_specs, out_specs=out_specs, check_vma=False)
```

time: 130 us -> 31.5 us (0.24)
  the two profiles are of different devices: /device:TPU:0 before, /device:TPU:2 now
where the time goes in v1:
time: 31.5 us; the launch traced here: 31.1 us
  Pallas kernels  23.9 us (76%)
  local copies, waits for them, and re-layouts  6.53 us (21%)
  between operations  0.68 us (2%)
    pallas_call x1, Pallas kernels, body(): pl.pallas_call(functools.partial(kernel, n_seq, n_res, sizes), out_shape=...  23.9 us
    unnamed x22, local copies, waits for them, and re-layouts  6.53 us

profile of v1, /device:TPU:2, one launch (start us, length us, event | category | flops | bytes accessed | tf_op | source)
XLA Modules:
  0.0 31.1 jit_solution(15302737627166649483)
XLA Ops:
  0.6 0.0 copy-start.8
  0.6 0.0 copy-start.5
  0.7 0.0 copy-start.7
  0.7 0.8 %copy.12.mask_ref = s32[32,16]{1,0:T(8,128)S(1)} copy(s32[32,16]{0,1:T(8,128)} %param.11) | data formatting | bytes 4096 | tf_op args[1]
  1.4 0.0 copy-done.8
  1.5 0.0 copy-start.3
  1.5 0.0 copy-start.4
  1.5 0.1 copy.13.wb_ref
  1.6 0.0 copy-done.5
  1.6 0.0 copy-done.7
  1.6 0.6 %copy-done.3 = f32[66,128]{1,0:T(8,128)S(1)} copy-done((f32[66,128]{1,0:T(8,128)S(1)}, f32[66,128]{1,0:T(8,128)}, u32[]{:S(2)}) %copy-start.3) | copy-done | bytes 33816
  2.2 0.0 copy-done.4
  2.2 0.0 copy-start
  2.2 1.0 %copy-done = f32[1024,128]{1,0:T(8,128)S(1)} copy-done((f32[1024,128]{1,0:T(8,128)S(1)}, f32[1024,128]{1,0:T(8,128)}, u32[]{:S(2)}) %copy-start) | copy-done | bytes 524312
  3.3 0.0 copy-start.1
  3.3 0.9 %copy-done.1 = f32[32,16,64]{2,1,0:T(8,128)S(1)} copy-done((f32[32,16,64]{2,1,0:T(8,128)S(1)}, f32[32,16,64]{2,1,0:T(8,128)}, u32[]{:S(2)}) %copy-start.1) | copy-done | bytes 131096
  4.2 0.0 copy-start.2
  4.2 0.9 %copy-done.2 = f32[16,16,128]{2,1,0:T(8,128)S(1)} copy-done((f32[16,16,128]{2,1,0:T(8,128)S(1)}, f32[16,16,128]{2,1,0:T(8,128)}, u32[]{:S(2)}) %copy-start.2) | copy-done | bytes 131096
  5.1 0.0 copy-start.6
  5.1 0.7 %copy-done.6 = bf16[64,64]{1,0:T(8,128)(2,1)S(1)} copy-done((bf16[64,64]{1,0:T(8,128)(2,1)S(1)}, bf16[64,64]{1,0:T(8,128)(2,1)}, u32[]{:S(2)}) %copy-start.6) | copy-done | bytes 8216
  5.8 23.9 %shard_map.113 = (f32[256,128]{1,0:T(8,128)S(1)}, f32[512,64]{1,0:T(8,128)S(1)}) custom-call(f32[512,64]{1,0:T(8,128)S(1)} %bitcast.5, s32[32,16]{1,0:T(8,128)S(1)} %copy.12.mask_ref, f32[256,128]{1,0:T(8,128)S(1)} %bitcast.7, s32[64]{0:T(128)S(1)} %copy-done.7, f32[66,128]{1,0:T(8,128)S(1)} %copy-done.3, bf16[64,64]{1,0:T(8,128)(2,1)S(1)} %copy-done.5, ...), custom_call_target="tpu_custom_call" | custom-call | tf_op jit(solution)/shard_map/pallas_call | solution.py:413
  29.7 0.7 %copy.16 = f32[16,16,128]{2,1,0:T(8,128)} copy(f32[16,16,128]{2,1,0:T(8,128)S(1)} %bitcast.6) | data formatting | bytes 262144
  30.4 0.7 %copy.17 = f32[32,16,64]{2,1,0:T(8,128)} copy(f32[32,16,64]{2,1,0:T(8,128)S(1)} %bitcast.4) | data formatting | bytes 262144
Async XLA Ops:
  0.6 0.8 %copy-start.8 = (f32[128,8]{0,1:T(8,128)S(1)}, f32[128,8]{0,1:T(8,128)}, u32[]{:S(2)}) copy-start(f32[128,8]{0,1:T(8,128)} %param.17) | copy-start | bytes 12292
  0.6 0.9 %copy-start.5 = (bf16[64,64]{1,0:T(8,128)(2,1)S(1)}, bf16[64,64]{1,0:T(8,128)(2,1)}, u32[]{:S(2)}) copy-start(bf16[64,64]{1,0:T(8,128)(2,1)} %wf_ref.1) | copy-start | bytes 24580
  0.7 0.9 %copy-start.7 = (s32[64]{0:T(128)S(1)}, s32[64]{0:T(128)}, u32[]{:S(2)}) copy-start(s32[64]{0:T(128)} %chain_ref.1) | copy-start | bytes 772
  1.5 0.8 %copy-start.3 = (f32[66,128]{1,0:T(8,128)S(1)}, f32[66,128]{1,0:T(8,128)}, u32[]{:S(2)}) copy-start(f32[66,128]{1,0:T(8,128)} %table_ref.1) | copy-start | bytes 101380
  1.5 0.8 %copy-start.4 = (bf16[64,256]{1,0:T(8,128)(2,1)S(1)}, bf16[64,256]{1,0:T(8,128)(2,1)}, u32[]{:S(2)}) copy-start(bf16[64,256]{1,0:T(8,128)(2,1)} %wa_ref.1) | copy-start | bytes 98308
  2.2 1.0 %copy-start = (f32[1024,128]{1,0:T(8,128)S(1)}, f32[1024,128]{1,0:T(8,128)}, u32[]{:S(2)}) copy-start(f32[1024,128]{1,0:T(8,128)} %wo_ref.1) | copy-start | bytes 1572868
  3.3 0.9 %copy-start.1 = (f32[32,16,64]{2,1,0:T(8,128)S(1)}, f32[32,16,64]{2,1,0:T(8,128)}, u32[]{:S(2)}) copy-start(f32[32,16,64]{2,1,0:T(8,128)} %param.10) | copy-start | bytes 393220
  4.2 0.9 %copy-start.2 = (f32[16,16,128]{2,1,0:T(8,128)S(1)}, f32[16,16,128]{2,1,0:T(8,128)}, u32[]{:S(2)}) copy-start(f32[16,16,128]{2,1,0:T(8,128)} %param.12) | copy-start | bytes 393220
  5.1 0.7 %copy-start.6 = (bf16[64,64]{1,0:T(8,128)(2,1)S(1)}, bf16[64,64]{1,0:T(8,128)(2,1)}, u32[]{:S(2)}) copy-start(bf16[64,64]{1,0:T(8,128)(2,1)} %wout_ref.1) | copy-start | bytes 24580

commit v2 on v1

--- a/solution.py
+++ b/solution.py
@@ -42,6 +42,18 @@
     n_seq,
     n_res,
     sizes,
+    align_hbm,
+    mask_hbm,
+    pair_hbm,
+    chain_hbm,
+    table_hbm,
+    wf_hbm,
+    wo_hbm,
+    wb_hbm,
+    wa_hbm,
+    wout_hbm,
+    pair_out,
+    align_out,
     align_ref,
     mask_ref,
     pair_ref,
@@ -52,8 +64,7 @@
     wb_ref,
     wa_ref,
     wout_ref,
-    pair_out,
-    align_out,
+    load_sem,
     x_scr,
     left_buf,
     right_buf,
@@ -98,6 +109,26 @@
     owner = q // ratio
     diagonal = (owner == r).astype(jnp.int32)
 
+    loads = [
+        pltpu.make_async_copy(source, target, load_sem.at[index])
+        for index, (source, target) in enumerate(
+            (
+                (align_hbm, align_ref),
+                (mask_hbm, mask_ref),
+                (wf_hbm, wf_ref),
+                (wo_hbm, wo_ref),
+                (wa_hbm, wa_ref),
+                (chain_hbm, chain_ref),
+                (table_hbm, table_ref),
+                (pair_hbm, pair_ref),
+                (wb_hbm, wb_ref),
+                (wout_hbm, wout_ref),
+            )
+        )
+    ]
+    for load in loads:
+        load.start()
+
     barrier = pltpu.get_barrier_semaphore()
     seq_peers = [lax.rem(q + d, n_seq) for d in range(n_seq)]
     res_peers = [lax.rem(r + d, n_res) for d in range(n_res)]
@@ -121,13 +152,15 @@
         else:
             greet()
 
+    for load in loads[:3]:
+        load.wait()
     normed = layer_norm(align_ref[...])
     x_scr[...] = normed
     half = rows // 2
     x_buf[r] = jnp.concatenate([normed[:half], normed[half:]], axis=1).astype(BF16)
-    mask = mask_ref[...].astype(F32)
+    mask_turned = mask_ref[...].astype(F32)
     eye = (iota((rd, rd), 0) == iota((rd, rd), 1)).astype(BF16)
-    mask_turned = dot(eye, mask.astype(BF16), ((1,), (1,)))
+    mask = dot(mask_turned.astype(BF16), eye, ((0,), (0,)))
     mask_wide = jnp.concatenate([mask_turned, jnp.zeros((rd, LANES - sd), F32)], axis=1)
     mask_buf[r] = mask_wide
     wf = wf_ref[...]
@@ -214,6 +247,8 @@
     def _():
         right_buf[q] = right_own[...]
 
+    for load in loads[3:]:
+        load.wait()
     wo_high, wo_low = split(wo_ref[...])
     wsplit[:, :cz] = wo_high
     wsplit[:, cz:] = wo_low
@@ -247,7 +282,7 @@
         )
 
     spread = (iota((heads, LANES), 1) // rd == iota((heads, LANES), 0)).astype(F32)
-    wb_high, wb_low = split(dot(wb_ref[...], spread, precision=PRECISE))
+    wb_high, wb_low = split(dot(wb_ref[...], spread, ((0,), (0,)), PRECISE))
     wb_both = jnp.concatenate([wb_high, wb_low], axis=1)
 
     def project(block):
@@ -408,7 +443,7 @@
         slot = max(cb, 8)
         sizes = (sd, rd, ch, cb, cz, co, heads, inner // heads, bins)
         vmem = pl.BlockSpec(memory_space=pltpu.VMEM)
-        smem = pl.BlockSpec(memory_space=pltpu.SMEM)
+        hbm = pl.BlockSpec(memory_space=pltpu.HBM)
         dma = pltpu.SemaphoreType.DMA
         pair_next, align_next = pl.pallas_call(
             functools.partial(kernel, n_seq, n_res, sizes),
@@ -416,9 +451,20 @@
                 jax.ShapeDtypeStruct((pairs, cz), F32),
                 jax.ShapeDtypeStruct((rows, ch), F32),
             ),
-            in_specs=[vmem, vmem, vmem, smem] + [vmem] * 6,
+            in_specs=[hbm] * 10,
             out_specs=(vmem, vmem),
             scratch_shapes=[
+                pltpu.VMEM((rows, ch), F32),
+                pltpu.VMEM((rd, sd), jnp.int32),
+                pltpu.VMEM((pairs, cz), F32),
+                pltpu.SMEM((residues,), jnp.int32),
+                pltpu.VMEM((bins, cz), F32),
+                pltpu.VMEM((ch, 2 * co), BF16),
+                pltpu.VMEM((co * co, cz), F32),
+                pltpu.VMEM((heads, cz), F32),
+                pltpu.VMEM((ch, 4 * inner), BF16),
+                pltpu.VMEM((inner, ch), BF16),
+                dma((10,)),
                 pltpu.VMEM((rows, ch), F32),
                 pltpu.VMEM((n_seq, sd, fl + LANES), BF16),
                 pltpu.VMEM((n_seq, sd, fl + LANES), BF16),
@@ -452,17 +498,17 @@
                 dma((n_seq,)),
             ],
             compiler_params=pltpu.CompilerParams(
-                collective_id=0, has_side_effects=True, vmem_limit_bytes=48 * 1024 * 1024
+                collective_id=0, has_side_effects=True, vmem_limit_bytes=64 * 1024 * 1024 - 65536
             ),
         )(
             align.reshape(rows, ch),
-            mask,
+            mask.T,
             pair.reshape(pairs, cz),
             chain,
             table,
             w_factors,
             w_outer,
-            w_bias,
+            w_bias.T,
             w_attention,
             w_output,
         )

time: 31.5 us -> 27.3 us (0.87)
  local copies, waits for them, and re-layouts: 6.53 us -> 2.32 us
    unnamed x22 -> x4, local copies, waits for them, and re-layouts: 6.53 us -> 2.32 us
where the time goes in v2:
time: 27.3 us; the launch traced here: 27.2 us
  Pallas kernels  24.2 us (89%)
  local copies, waits for them, and re-layouts  2.32 us (8%)
  between operations  0.65 us (2%)
    pallas_call x1, Pallas kernels, body(): pl.pallas_call(functools.partial(kernel, n_seq, n_res, sizes), out_shape=...  24.2 us
    unnamed x4, local copies, waits for them, and re-layouts  2.32 us

profile of v2, /device:TPU:2, one launch (start us, length us, event | category | flops | bytes accessed | tf_op | source)
XLA Modules:
  0.0 27.2 jit_solution(8689377088870559389)
XLA Ops:
  0.6 24.2 %shard_map.113 = (f32[256,128]{1,0:T(8,128)}, f32[512,64]{1,0:T(8,128)}) custom-call(f32[512,64]{1,0:T(8,128)} %bitcast.6, s32[16,32]{1,0:T(8,128)} %bitcast.10, f32[256,128]{1,0:T(8,128)} %bitcast.8, s32[64]{0:T(128)} %chain_hbm.1, f32[66,128]{1,0:T(8,128)} %table_hbm.1, bf16[64,64]{1,0:T(8,128)(2,1)} %wf_hbm.1, f32[1024,128]{1,0:T(8,128)} %wo_hbm.1, ...), custom_call_target="tpu_custom_call" | custom-call | tf_op jit(solution)/shard_map/pallas_call | solution.py:448
  24.8 0.0 copy-start
  24.8 1.6 %copy.14 = f32[16,16,128]{2,1,0:T(8,128)} copy(f32[16,16,128]{2,1,0:T(8,128)} %bitcast.9) | data formatting | bytes 262144
  26.5 0.0 copy-done
  26.5 0.7 %copy.15 = f32[32,16,64]{2,1,0:T(8,128)} copy(f32[32,16,64]{2,1,0:T(8,128)S(1)} %bitcast.7) | data formatting | bytes 262144
Async XLA Ops:
  24.8 1.6 %copy-start = (f32[512,64]{1,0:T(8,128)S(1)}, f32[512,64]{1,0:T(8,128)}, u32[]{:S(2)}) copy-start(f32[512,64]{1,0:T(8,128)} %get-tuple-element.5) | copy-start | bytes 393220

commit v3 on v2

--- a/solution.py
+++ b/solution.py
@@ -89,6 +89,7 @@
     send_l,
     recv_l,
     send_r,
+    send_f,
     recv_r,
     send_x,
     recv_x,
@@ -107,7 +108,9 @@
     q = lax.axis_index("seq")
     r = lax.axis_index("res")
     owner = q // ratio
-    diagonal = (owner == r).astype(jnp.int32)
+    relay = lax.rem(q, n_res)
+    own_slot = jnp.logical_and(owner == r, relay == r)
+    diagonal = own_slot.astype(jnp.int32)
 
     loads = [
         pltpu.make_async_copy(source, target, load_sem.at[index])
@@ -140,17 +143,18 @@
         pl.semaphore_signal(
             barrier, inc=1, device_id={"seq": q, "res": res_peers[d]}, device_id_type=MESH
         )
-    for d in range(n_seq):
-
-        def greet(d=d):
+    shares = n_seq // n_res
+    for u in range(shares):
+
+        def greet(u=u):
             pl.semaphore_signal(
-                barrier, inc=1, device_id={"seq": seq_peers[d], "res": owner}, device_id_type=MESH
+                barrier,
+                inc=1,
+                device_id={"seq": u * n_res + r, "res": owner},
+                device_id_type=MESH,
             )
 
-        if d == 0:
-            pl.when(owner != r)(greet)
-        else:
-            greet()
+        pl.when(jnp.logical_or(owner != r, u * n_res + r != q))(greet)
 
     for load in loads[:3]:
         load.wait()
@@ -186,17 +190,38 @@
     left_buf[q, :, fl : fl + LANES] = mask_pad
     right_own[:, fl : fl + LANES] = mask_pad
 
-    pl.semaphore_wait(barrier, (n_seq - 1) + (n_res - 1) + ratio * n_res - diagonal)
-
-    def right_copy(t, d):
+    pl.semaphore_wait(barrier, (n_seq - 1) + (n_res - 1) + ratio - diagonal)
+
+    def right_copy(t):
         return pltpu.make_async_remote_copy(
             src_ref=right_own,
             dst_ref=right_buf.at[q],
-            send_sem=send_r.at[t * n_res + d],
+            send_sem=send_r.at[t],
             recv_sem=recv_r.at[q],
-            device_id={"seq": r * ratio + t, "res": res_peers[d]},
-            device_id_type=MESH,
-        )
+            device_id={"seq": r * ratio + t, "res": relay},
+            device_id_type=MESH,
+        )
+
+    def forward_copy(u, d):
+        slot = u * n_res + r
+        return pltpu.make_async_remote_copy(
+            src_ref=right_buf.at[slot],
+            dst_ref=right_buf.at[slot],
+            send_sem=send_f.at[u * n_res + d],
+            recv_sem=recv_r.at[slot],
+            device_id={"seq": q, "res": res_peers[d]},
+            device_id_type=MESH,
+        )
+
+    def right_arrival(slot):
+        pltpu.make_async_remote_copy(
+            src_ref=right_own,
+            dst_ref=right_buf.at[slot],
+            send_sem=send_r.at[0],
+            recv_sem=recv_r.at[slot],
+            device_id={"seq": q, "res": res_peers[1]},
+            device_id_type=MESH,
+        ).wait_recv()
 
     def left_copy(d):
         return pltpu.make_async_remote_copy(
@@ -230,20 +255,13 @@
 
     def each_right(action):
         for t in range(ratio):
-            for d in range(n_res):
-                if d == 0:
-                    pl.when(r * ratio + t != q)(functools.partial(action, t, d))
-                else:
-                    action(t, d)
-
-    each_right(lambda t, d: right_copy(t, d).start())
+            pl.when(jnp.logical_or(relay != r, r * ratio + t != q))(functools.partial(action, t))
+
+    each_right(lambda t: right_copy(t).start())
     for d in range(1, n_seq):
         left_copy(d).start()
-    for d in range(1, n_res):
-        x_copy(d).start()
-        mask_copy(d).start()
-
-    @pl.when(owner == r)
+
+    @pl.when(own_slot)
     def _():
         right_buf[q] = right_own[...]
 
@@ -255,6 +273,15 @@
     wa_diag[...] = jnp.zeros_like(wa_diag)
     wa_diag[:ch, : 4 * inner] = wa_ref[...]
     wa_diag[ch:, 4 * inner :] = wa_ref[...]
+
+    for u in range(shares):
+        slot = u * n_res + r
+        pl.when(jnp.logical_or(owner != r, slot != q))(functools.partial(right_arrival, slot))
+        for d in range(1, n_res):
+            forward_copy(u, d).start()
+    for d in range(1, n_res):
+        x_copy(d).start()
+        mask_copy(d).start()
 
     row = iota((rd, LANES), 0)
     lane = iota((rd, LANES), 1)
@@ -306,19 +333,9 @@
 
     for d in range(1, n_seq):
         left_copy(d).wait_recv()
-    for source in range(n_seq):
-
-        def arrive(source=source):
-            pltpu.make_async_remote_copy(
-                src_ref=right_own,
-                dst_ref=right_buf.at[source],
-                send_sem=send_r.at[0],
-                recv_sem=recv_r.at[source],
-                device_id={"seq": source, "res": owner},
-                device_id_type=MESH,
-            ).wait_recv()
-
-        pl.when(jnp.logical_or(owner != r, q != source))(arrive)
+    for d in range(1, n_res):
+        for u in range(shares):
+            right_arrival(u * n_res + res_peers[d])
 
     left_all = left_buf[:, :, :fl].reshape(n_seq * sd, fl)
     block = iota((rd, LANES), 1) // co
@@ -418,7 +435,10 @@
     gated = (gate_scr[...] * att_scr[...]).astype(BF16)[:, :inner]
     align_out[...] = align_ref[...] + dot(gated, wout_ref[...])
 
-    each_right(lambda t, d: right_copy(t, d).wait_send())
+    each_right(lambda t: right_copy(t).wait_send())
+    for u in range(shares):
+        for d in range(1, n_res):
+            forward_copy(u, d).wait_send()
     for d in range(1, n_seq):
         left_copy(d).wait_send()
         bias_copy(d).wait_send()
@@ -488,7 +508,8 @@
                 pltpu.VMEM((sd, residues, LANES), F32),
                 dma((n_seq,)),
                 dma((n_seq,)),
-                dma((rd // cb * n_res,)),
+                dma((rd // cb,)),
+                dma((n_seq,)),
                 dma((n_seq,)),
                 dma((n_res,)),
                 dma((n_res,)),

time: 27.3 us -> 22.8 us (0.84)
  the two profiles are of different devices: /device:TPU:2 before, /device:TPU:0 now
where the time goes in v3:
time: 22.8 us; the launch traced here: 22.6 us
  Pallas kernels  19.6 us (86%)
  local copies, waits for them, and re-layouts  2.32 us (10%)
  between operations  0.65 us (3%)
    pallas_call x1, Pallas kernels, body(): pl.pallas_call(functools.partial(kernel, n_seq, n_res, sizes), out_shape=...  19.6 us
    unnamed x4, local copies, waits for them, and re-layouts  2.32 us

profile of v3, /device:TPU:0, one launch (start us, length us, event | category | flops | bytes accessed | tf_op | source)
XLA Modules:
  0.0 22.6 jit_solution(1969818955285468450)
XLA Ops:
  0.6 19.6 %shard_map.113 = (f32[256,128]{1,0:T(8,128)}, f32[512,64]{1,0:T(8,128)}) custom-call(f32[512,64]{1,0:T(8,128)} %bitcast.6, s32[16,32]{1,0:T(8,128)} %bitcast.10, f32[256,128]{1,0:T(8,128)} %bitcast.8, s32[64]{0:T(128)} %chain_hbm.1, f32[66,128]{1,0:T(8,128)} %table_hbm.1, bf16[64,64]{1,0:T(8,128)(2,1)} %wf_hbm.1, f32[1024,128]{1,0:T(8,128)} %wo_hbm.1, ...), custom_call_target="tpu_custom_call" | custom-call | tf_op jit(solution)/shard_map/pallas_call | solution.py:468
  20.3 0.0 copy-start
  20.3 1.6 %copy.14 = f32[16,16,128]{2,1,0:T(8,128)} copy(f32[16,16,128]{2,1,0:T(8,128)} %bitcast.9) | data formatting | bytes 262144
  21.9 0.0 copy-done
  21.9 0.7 %copy.15 = f32[32,16,64]{2,1,0:T(8,128)} copy(f32[32,16,64]{2,1,0:T(8,128)S(1)} %bitcast.7) | data formatting | bytes 262144
Async XLA Ops:
  20.3 1.6 %copy-start = (f32[512,64]{1,0:T(8,128)S(1)}, f32[512,64]{1,0:T(8,128)}, u32[]{:S(2)}) copy-start(f32[512,64]{1,0:T(8,128)} %get-tuple-element.5) | copy-start | bytes 393220

commit v4 on v3

--- a/solution.py
+++ b/solution.py
@@ -52,8 +52,11 @@
     wb_hbm,
     wa_hbm,
     wout_hbm,
+    pair_hbm_out,
+    align_hbm_out,
     pair_out,
     align_out,
+    store_sem,
     align_ref,
     mask_ref,
     pair_ref,
@@ -379,6 +382,8 @@
     pair_next = base_scr[...] + update * scale
     for j in range(cb):
         pair_out[pl.ds(j, rd, stride=cb), :] = pair_next[j * rd : (j + 1) * rd]
+    pair_store = pltpu.make_async_copy(pair_out, pair_hbm_out, store_sem.at[0])
+    pair_store.start()
     n_high, n_low = split(layer_norm(pair_next))
     both = dot(n_high, wb_both)
     head = both[:, :LANES] + both[:, LANES:] + dot(n_low, wb_high)
@@ -434,6 +439,9 @@
         att_scr[at] = jnp.sum(mixed.reshape(heads, rd, LANES), axis=0)
     gated = (gate_scr[...] * att_scr[...]).astype(BF16)[:, :inner]
     align_out[...] = align_ref[...] + dot(gated, wout_ref[...])
+    align_store = pltpu.make_async_copy(align_out, align_hbm_out, store_sem.at[1])
+    align_store.start()
+    pair_store.wait()
 
     each_right(lambda t: right_copy(t).wait_send())
     for u in range(shares):
@@ -445,6 +453,7 @@
     for d in range(1, n_res):
         x_copy(d).wait_send()
         mask_copy(d).wait_send()
+    align_store.wait()
 
 
 def solution(mesh):
@@ -462,7 +471,6 @@
         per = LANES // co
         slot = max(cb, 8)
         sizes = (sd, rd, ch, cb, cz, co, heads, inner // heads, bins)
-        vmem = pl.BlockSpec(memory_space=pltpu.VMEM)
         hbm = pl.BlockSpec(memory_space=pltpu.HBM)
         dma = pltpu.SemaphoreType.DMA
         pair_next, align_next = pl.pallas_call(
@@ -472,8 +480,11 @@
                 jax.ShapeDtypeStruct((rows, ch), F32),
             ),
             in_specs=[hbm] * 10,
-            out_specs=(vmem, vmem),
+            out_specs=(hbm, hbm),
             scratch_shapes=[
+                pltpu.VMEM((pairs, cz), F32),
+                pltpu.VMEM((rows, ch), F32),
+                dma((2,)),
                 pltpu.VMEM((rows, ch), F32),
                 pltpu.VMEM((rd, sd), jnp.int32),
                 pltpu.VMEM((pairs, cz), F32),

time: 22.8 us -> 22.7 us (level)
  no operation moved by 1% of the time
where the time goes in v4:
time: 22.7 us; the launch traced here: 22.6 us
  Pallas kernels  19.6 us (86%)
  local copies, waits for them, and re-layouts  2.32 us (10%)
  between operations  0.65 us (3%)
    pallas_call x1, Pallas kernels, body(): pl.pallas_call(functools.partial(kernel, n_seq, n_res, sizes), out_shape=...  19.6 us
    unnamed x4, local copies, waits for them, and re-layouts  2.32 us

profile of v4, /device:TPU:0, one launch (start us, length us, event | category | flops | bytes accessed | tf_op | source)
XLA Modules:
  0.0 22.6 jit_solution(15083350549525797254)
XLA Ops:
  0.6 19.6 %shard_map.113 = (f32[256,128]{1,0:T(8,128)}, f32[512,64]{1,0:T(8,128)}) custom-call(f32[512,64]{1,0:T(8,128)} %bitcast.6, s32[16,32]{1,0:T(8,128)} %bitcast.10, f32[256,128]{1,0:T(8,128)} %bitcast.8, s32[64]{0:T(128)} %chain_hbm.1, f32[66,128]{1,0:T(8,128)} %table_hbm.1, bf16[64,64]{1,0:T(8,128)(2,1)} %wf_hbm.1, f32[1024,128]{1,0:T(8,128)} %wo_hbm.1, ...), custom_call_target="tpu_custom_call" | custom-call | tf_op jit(solution)/shard_map/pallas_call | solution.py:476
  20.2 0.0 copy-start
  20.2 1.6 %copy.14 = f32[16,16,128]{2,1,0:T(8,128)} copy(f32[16,16,128]{2,1,0:T(8,128)} %bitcast.9) | data formatting | bytes 262144
  21.8 0.0 copy-done
  21.9 0.7 %copy.15 = f32[32,16,64]{2,1,0:T(8,128)} copy(f32[32,16,64]{2,1,0:T(8,128)S(1)} %bitcast.7) | data formatting | bytes 262144
Async XLA Ops:
  20.2 1.6 %copy-start = (f32[512,64]{1,0:T(8,128)S(1)}, f32[512,64]{1,0:T(8,128)}, u32[]{:S(2)}) copy-start(f32[512,64]{1,0:T(8,128)} %get-tuple-element.5) | copy-start | bytes 393220
